TPU v7x, 32 devices: a whole 2x2x4 slice. The times are simulated.
32 devices in a mesh: section: 4 (over z), ctx: 4 (over x, core), dp: 2 (over y).
Axes of the slice: x: 2, y: 2, z: 4, core: 2. Of those that a mesh axis runs over, the one named last changes fastest.
Arguments:
- stream: bfloat16 [4, 256, 8192], P('section', 'dp', 'ctx'), may hold values from -6 to 6
- norm_gain: float32 [4, 8192], P('section', 'ctx'), may hold values from 0.5 to 2
- w_router: bfloat16 [4, 8192], P('section', 'ctx'), may hold values from -0.0625 to 0.0625
- w_gate: bfloat16 [4, 8192, 14336], P('section', 'ctx', 'dp'), may hold values from -0.0625 to 0.0625
- w_up: bfloat16 [4, 8192, 14336], P('section', 'ctx', 'dp'), may hold values from -0.0625 to 0.0625
- w_down: bfloat16 [4, 14336, 8192], P('section', 'dp', 'ctx'), may hold values from -0.046875 to 0.046875
- keep_rows: int32 [2, 4, 2, 32], P(None, 'section', 'dp'), may hold values from -1 to 127, as said below
Outputs:
- advanced: bfloat16 [4, 256, 8192], P('section', 'dp', 'ctx')
Inputs may be any that keep to these rules, and one draw needn't show every extreme that they name: `keep_rows`: each list holds distinct row indices first, then -1 in its empty slots. Over the 2 lists of one tick and section exactly 32 rows are kept; in each tick and section some list is full and some is empty.
All inputs are finite; a program needn't handle non-finite values.
Results may differ from a plain program's by a relative error of at most 0.005.
Values may be sent and summed in bfloat16 or wider, within the bound.
A program may use at most 192 MiB of HBM per device.

v0:
```python
import jax
import jax.numpy as jnp
from jax import lax
from jax.sharding import PartitionSpec as P

D = 8192


eps = 1e-05


def from_behind(value, axis, steps):
    count = lax.axis_size(axis)
    pairs = [(source, (source + steps) % count) for source in range(count)]
    return lax.ppermute(value, axis, pairs)


def hidden_block(normed, w_gate, w_up, w_down):
    row_piece = lax.all_gather(normed, "dp", axis=0, tiled=True)
    gate_part = jnp.dot(row_piece, w_gate, preferred_element_type=jnp.float32)
    up_part = jnp.dot(row_piece, w_up, preferred_element_type=jnp.float32)
    partial_value = jnp.stack([gate_part, up_part], axis=1)
    summed = lax.psum(partial_value, "ctx")
    hidden = (jax.nn.silu(summed[:, 0]) * summed[:, 1]).astype(jnp.bfloat16)
    return lax.psum_scatter(
        jnp.dot(hidden, w_down, preferred_element_type=jnp.float32).astype(jnp.bfloat16),
        "dp",
        scatter_dimension=0,
        tiled=True,
    ).astype(jnp.float32)


def routed_layer(stream, keep_list, gain_row, router, w_gate, w_up, w_down):
    is_kept = keep_list >= 0
    picked = jnp.take(stream, jnp.maximum(keep_list, 0), axis=0)
    rows_wide = picked.astype(jnp.float32)
    squares = jnp.sum(rows_wide * rows_wide, axis=1)
    logits = jnp.sum(rows_wide * router.astype(jnp.float32)[None, :], axis=1)
    squares, logits = lax.psum((squares, logits), "ctx")
    scaling = lax.rsqrt(squares / D + eps)
    normed = jnp.where(
        is_kept[:, None], rows_wide * scaling[:, None] * gain_row[None, :], 0.0
    ).astype(jnp.bfloat16)
    update = hidden_block(normed, w_gate, w_up, w_down)
    new_rows = (rows_wide + jax.nn.sigmoid(logits)[:, None] * update).astype(jnp.bfloat16)
    target = jnp.where(is_kept, keep_list, stream.shape[0])
    return stream.at[target].set(new_rows, mode="drop")


def local(stream, norm_gain, w_router, w_gate, w_up, w_down, keep_rows):
    first_pass = routed_layer(
        stream[0], keep_rows[0, 0, 0], norm_gain[0], w_router[0], w_gate[0], w_up[0], w_down[0]
    )
    passed = from_behind(first_pass, "section", 1)
    second_pass = routed_layer(
        passed, keep_rows[1, 0, 0], norm_gain[0], w_router[0], w_gate[0], w_up[0], w_down[0]
    )
    section_place = lax.axis_index("section")
    result = jnp.where(section_place == 0, passed, second_pass)
    return result[None]


def solution(mesh):
    return jax.shard_map(
        local,
        mesh=mesh,
        in_specs=(
            P("section", "dp", "ctx"),
            P("section", "ctx"),
            P("section", "ctx"),
            P("section", "ctx", "dp"),
            P("section", "ctx", "dp"),
            P("section", "dp", "ctx"),
            P(None, "section", "dp", None),
        ),
        out_specs=P("section", "dp", "ctx"),
        check_vma=False,
    )
```

profile of v0, /device:TPU:0, one launch (start us, length us, event | category | flops | bytes accessed | tf_op | source)
XLA Modules:
  0.0 325.9 jit_solution(13672440571319732338)
XLA Ops:
  6.5 1.0 copy.13
  8.9 0.7 mul.113
  10.5 8.3 %all-reduce.1 = (f32[32]{0:T(128)S(1)}, f32[32]{0:T(128)S(1)}) all-reduce(f32[32]{0:T(128)S(1)} %get-tuple-element.9, f32[32]{0:T(128)S(1)} %get-tuple-element.8), channel_id=1, replica_groups=mesh['section'=4,'ctx'=4,'dp'=2] {'ctx'}, use_global_device_ids=true, to_apply=%region_3.5 | all-reduce | flops 64 | bytes 512 | tf_op jit(solution)/shard_map/psum | solution.py:39
  18.9 0.8 fusion.40
  19.7 5.6 %all_gather.6 = bf16[64,2048]{1,0:T(8,128)(2,1)S(1)} all-gather(bf16[32,2048]{1,0:T(8,128)(2,1)S(1)} %fusion.40), channel_id=1, replica_groups=mesh['section'=4,'ctx'=4,'dp'=2] {'dp'}, dimensions={0}, use_global_device_ids=true | all-gather | bytes 393216 | tf_op jit(solution)/shard_map/all_gather | solution.py:19
  25.4 12.0 %fusion.12 = f32[64,1,7168]{2,0,1:T(8,128)S(1)} fusion(bf16[64,2048]{1,0:T(8,128)(2,1)S(1)} %all_gather.6, bf16[1,2048,7168]{2,1,0:T(8,128)(2,1)} %param.12), kind=kOutput, calls=%fused_computation.16 | convolution fusion | flops 1879048192 | bytes 31457280 | tf_op jit(solution)/shard_map/dot_general | solution.py:20
  37.3 12.0 %fusion.18 = f32[64,1,7168]{2,0,1:T(8,128)S(1)} fusion(bf16[64,2048]{1,0:T(8,128)(2,1)S(1)} %all_gather.6, bf16[1,2048,7168]{2,1,0:T(8,128)(2,1)} %param.13), kind=kOutput, calls=%fused_computation.18 | convolution fusion | flops 1879048192 | bytes 31457280 | tf_op jit(solution)/shard_map/dot_general | solution.py:21
  49.3 2.1 pad_maximum_fusion
  51.5 77.4 %all-reduce.5.cloned.1.call-done = f32[64,2,7168]{2,0,1:T(8,128)} async-done(((f32[64,2,7168]{2,0,1:T(8,128)}), f32[64,2,7168]{2,0,1:T(8,128)}) %all-reduce.5.cloned.1.call-update) | async-done | bytes 3670032 | tf_op jit(solution)/shard_map/psum | solution.py:23
  128.9 16.4 %fusion.24 = bf16[64,2048]{1,0:T(8,128)(2,1)} fusion(bf16[1,7168,2048]{2,1,0:T(8,128)(2,1)} %param.14, f32[64,2,7168]{2,0,1:T(8,128)} %all-reduce.5.cloned.1.call-done), kind=kOutput, calls=%fused_computation.22 | convolution fusion | flops 1881931776 | bytes 33292288 | tf_op jit(solution)/shard_map/dot_general | solution.py:26
  145.4 11.9 %reduce-scatter.3.cloned.1.call-done = bf16[32,2048]{1,0:T(8,128)(2,1)} async-done(((bf16[64,2048]{1,0:T(8,128)(2,1)}), bf16[32,2048]{1,0:T(8,128)(2,1)}) %reduce-scatter.3.cloned.1.call-update) | async-done | bytes 131088 | tf_op jit(solution)/shard_map/reduce_scatter | solution.py:25
  157.3 1.6 scatter_custom_fusion
  158.9 1.5 collective-permute-start
  160.4 14.0 %collective-permute-done = bf16[128,2048]{1,0:T(8,128)(2,1)S(1)} collective-permute-done((bf16[128,2048]{1,0:T(8,128)(2,1)S(1)}, bf16[128,2048]{1,0:T(8,128)(2,1)S(1)}, u32[]{:S(2)}, u32[]{:S(2)}) %collective-permute-start) | collective-permute-done | bytes 524320 | tf_op jit(solution)/shard_map/ppermute | solution.py:15
  175.3 5.7 %all-reduce = (f32[32]{0:T(128)S(1)}, f32[32]{0:T(128)S(1)}) all-reduce(f32[32]{0:T(128)S(1)} %get-tuple-element.7, f32[32]{0:T(128)S(1)} %get-tuple-element.6), channel_id=1, replica_groups=mesh['section'=4,'ctx'=4,'dp'=2] {'ctx'}, use_global_device_ids=true, to_apply=%region_10.12 | all-reduce | flops 64 | bytes 512 | tf_op jit(solution)/shard_map/psum | solution.py:39
  181.1 6.1 %all_gather.7 = bf16[64,2048]{1,0:T(8,128)(2,1)S(1)} all-gather(bf16[32,2048]{1,0:T(8,128)(2,1)S(1)} %fusion.46), channel_id=1, replica_groups=mesh['section'=4,'ctx'=4,'dp'=2] {'dp'}, dimensions={0}, use_global_device_ids=true | all-gather | bytes 393216 | tf_op jit(solution)/shard_map/all_gather | solution.py:19
  187.2 12.0 %fusion.15 = f32[64,1,7168]{2,0,1:T(8,128)S(1)} fusion(bf16[64,2048]{1,0:T(8,128)(2,1)S(1)} %all_gather.7, bf16[1,2048,7168]{2,1,0:T(8,128)(2,1)} %param.12), kind=kOutput, calls=%fused_computation.17 | convolution fusion | flops 1879048192 | bytes 31457280 | tf_op jit(solution)/shard_map/dot_general | solution.py:20
  199.2 12.0 %fusion.21 = f32[64,1,7168]{2,0,1:T(8,128)S(1)} fusion(bf16[64,2048]{1,0:T(8,128)(2,1)S(1)} %all_gather.7, bf16[1,2048,7168]{2,1,0:T(8,128)(2,1)} %param.13), kind=kOutput, calls=%fused_computation.19 | convolution fusion | flops 1879048192 | bytes 31457280 | tf_op jit(solution)/shard_map/dot_general | solution.py:21
  211.2 2.1 pad_maximum_fusion.1
  213.4 75.2 %all-reduce.7.cloned.1.call-done = f32[64,2,7168]{2,0,1:T(8,128)} async-done(((f32[64,2,7168]{2,0,1:T(8,128)}), f32[64,2,7168]{2,0,1:T(8,128)}) %all-reduce.7.cloned.1.call-update) | async-done | bytes 3670032 | tf_op jit(solution)/shard_map/psum | solution.py:23
  288.6 16.4 %fusion.27 = bf16[64,2048]{1,0:T(8,128)(2,1)} fusion(bf16[1,7168,2048]{2,1,0:T(8,128)(2,1)} %param.14, f32[64,2,7168]{2,0,1:T(8,128)} %all-reduce.7.cloned.1.call-done), kind=kOutput, calls=%fused_computation.23 | convolution fusion | flops 1881931776 | bytes 33292288 | tf_op jit(solution)/shard_map/dot_general | solution.py:26
  305.1 11.9 %reduce-scatter.5.cloned.1.call-done = bf16[32,2048]{1,0:T(8,128)(2,1)} async-done(((bf16[64,2048]{1,0:T(8,128)(2,1)}), bf16[32,2048]{1,0:T(8,128)(2,1)}) %reduce-scatter.5.cloned.1.call-update) | async-done | bytes 131088 | tf_op jit(solution)/shard_map/reduce_scatter | solution.py:25
  316.9 1.6 scatter_custom_fusion.1
  318.5 0.9 select_bitcast_fusion
  (27 shorter events, 3.5 us)
Async XLA Ops:
  6.5 122.4 %all-reduce.5.cloned.1.call-start = ((), (), s32[]{:S(2)}) async-start(), calls=%async_computation.2 | async-start | bytes 7340032 | tf_op jit(solution)/shard_map/psum | solution.py:23
  51.5 93.9 %copy-start.1 = (s32[2,1,1,32]{3,2,1,0:T(1,128)S(1)}, s32[2,1,1,32]{3,2,1,0:T(1,128)}, u32[]{:S(2)}) copy-start(s32[2,1,1,32]{3,2,1,0:T(1,128)} %param.15) | copy-start | bytes 772
  51.5 129.5 %copy-start = (f32[1,2048]{1,0:T(1,128)S(1)}, f32[1,2048]{1,0:T(1,128)}, u32[]{:S(2)}) copy-start(f32[1,2048]{1,0:T(1,128)} %param.10) | copy-start | bytes 24580
  51.5 105.8 %reduce-scatter.3.cloned.1.call-start = ((), (), s32[]{:S(2)}) async-start(), calls=%async_computation.3 | async-start | bytes 393216 | tf_op jit(solution)/shard_map/reduce_scatter | solution.py:25
  145.3 143.3 %all-reduce.7.cloned.1.call-start = ((), (), s32[]{:S(2)}) async-start(), calls=%async_computation.4 | async-start | bytes 7340032 | tf_op jit(solution)/shard_map/psum | solution.py:23
  158.9 15.5 %collective-permute-start = (bf16[128,2048]{1,0:T(8,128)(2,1)S(1)}, bf16[128,2048]{1,0:T(8,128)(2,1)S(1)}, u32[]{:S(2)}, u32[]{:S(2)}) collective-permute-start(bf16[128,2048]{1,0:T(8,128)(2,1)S(1)} %scatter_custom_fusion), channel_id=1, source_target_pairs={{0,8},{8,16},{16,24},{24,0},{1,9},{9,17},{17,25},{25,1},{2,10},{10... | collective-permute-start | bytes 1572872 | tf_op jit(solution)/shard_map/ppermute | solution.py:15
  213.3 103.6 %reduce-scatter.5.cloned.1.call-start = ((), (), s32[]{:S(2)}) async-start(), calls=%async_computation.5 | async-start | bytes 393216 | tf_op jit(solution)/shard_map/reduce_scatter | solution.py:25
Sparse Core Ops, SparseCore 0:
  51.6 77.3 all-reduce.4
  145.5 11.7 reduce-scatter.2
  213.4 75.1 all-reduce.6
  305.1 11.7 reduce-scatter.4
where the time goes:
time: 326 us
  waiting for transfers between devices  190 us (58%)
  matrix products  80.7 us (25%)
  blocking collectives  25.8 us (8%)
  between operations  13.3 us (4%)
  other arithmetic  11.7 us (4%)
    psum x2, waiting for transfers between devices, hidden_block(): summed = lax.psum(partial_value, 'ctx')  153 us
    dot_general x2, matrix products, hidden_block(): jnp.dot(hidden, w_down, preferred_element_type=jnp.float32)  32.8 us
    dot_general x2, matrix products, hidden_block(): up_part = jnp.dot(row_piece, w_up, preferred_element_type=jnp.float32)  24 us
    dot_general x2, matrix products, hidden_block(): gate_part = jnp.dot(row_piece, w_gate, preferred_element_type=jnp.float32)  24 us
    reduce_scatter x2, waiting for transfers between devices, hidden_block(): lax.psum_scatter(jnp.dot(hidden, w_down, preferred_element_type=jnp.float...  23.7 us
    psum x2, blocking collectives, routed_layer(): squares, logits = lax.psum((squares, logits), 'ctx')  14 us
    ppermute x1, waiting for transfers between devices, from_behind(): return lax.ppermute(value, axis, pairs)  14 us
    all_gather x2, blocking collectives, hidden_block(): row_piece = lax.all_gather(normed, 'dp', axis=0, tiled=True)  11.7 us
  transfers between devices with their start and end apart: 5, of which 5 were waited for; matrix products, arithmetic and copies ran while one was open for 0% of the time, Pallas kernels for 0%

commit v1 on v0

v1 whole, which is shorter than its diff:
```python
import functools
import jax
import jax.numpy as jnp
from jax import lax
from jax.experimental import pallas as pl
from jax.experimental.pallas import tpu as pltpu
from jax.sharding import PartitionSpec as P

eps = 1e-05
F32, BF16 = jnp.float32, jnp.bfloat16
MESH = pl.DeviceIdType.MESH


def from_behind(value, axis, steps):
    count = lax.axis_size(axis)
    pairs = [(source, (source + steps) % count) for source in range(count)]
    return lax.ppermute(value, axis, pairs)


def hidden_block(normed, w_gate, w_up, w_down):
    row_piece = lax.all_gather(normed, "dp", axis=0, tiled=True)
    gate_part = jnp.dot(row_piece, w_gate, preferred_element_type=F32)
    up_part = jnp.dot(row_piece, w_up, preferred_element_type=F32)
    partial_value = jnp.stack([gate_part, up_part], axis=1)
    summed = lax.psum(partial_value, "ctx")
    hidden = (jax.nn.silu(summed[:, 0]) * summed[:, 1]).astype(BF16)
    return lax.psum_scatter(
        jnp.dot(hidden, w_down, preferred_element_type=F32).astype(BF16),
        "dp",
        scatter_dimension=0,
        tiled=True,
    ).astype(F32)


def routed_layer(stream, keep_list, gain_row, router, w_gate, w_up, w_down):
    width = stream.shape[1] * lax.axis_size("ctx")
    is_kept = keep_list >= 0
    picked = jnp.take(stream, jnp.maximum(keep_list, 0), axis=0)
    rows_wide = picked.astype(F32)
    squares = jnp.sum(rows_wide * rows_wide, axis=1)
    logits = jnp.sum(rows_wide * router.astype(F32)[None, :], axis=1)
    squares, logits = lax.psum((squares, logits), "ctx")
    scaling = lax.rsqrt(squares / width + eps)
    normed = jnp.where(
        is_kept[:, None], rows_wide * scaling[:, None] * gain_row[None, :], 0.0
    ).astype(BF16)
    update = hidden_block(normed, w_gate, w_up, w_down)
    new_rows = (rows_wide + jax.nn.sigmoid(logits)[:, None] * update).astype(BF16)
    target = jnp.where(is_kept, keep_list, stream.shape[0])
    return stream.at[target].set(new_rows, mode="drop")


def local(stream, norm_gain, w_router, w_gate, w_up, w_down, keep_rows):
    first_pass = routed_layer(
        stream[0], keep_rows[0, 0, 0], norm_gain[0], w_router[0], w_gate[0], w_up[0], w_down[0]
    )
    passed = from_behind(first_pass, "section", 1)
    second_pass = routed_layer(
        passed, keep_rows[1, 0, 0], norm_gain[0], w_router[0], w_gate[0], w_up[0], w_down[0]
    )
    section_place = lax.axis_index("section")
    result = jnp.where(section_place == 0, passed, second_pass)
    return result[None]


UK, UN = 1024, 512
HALF = UN // 2
STAY = 9
RING = 17
LAG = 3


def rc(src, dst, send, recv, where):
    return pltpu.make_async_remote_copy(
        src_ref=src, dst_ref=dst, send_sem=send, recv_sem=recv,
        device_id=where, device_id_type=MESH,
    )


def kernel(dims, stream, gain, router, keeps, wg, wu, wd, out, buf, pstream,
           klist, kprev, xsend, xrecv, xr, xg, stat_send, stat_recv, rs_b, sig_b,
           part, own, p1send, p1recv, p2send, p2recv, hid, usend, urecv, news,
           newr, b1send, b1recv, msend, mrecv,
           wsem, p1s, p1r, p2s, p2r, p3s, p3r, us, ur, ns, nr, sts, strv,
           misc_s, misc_r):
    n_sec, cap, tok, feat, ff, width = dims
    kh = feat // UK
    nj = ff // UN
    nn = feat // UN
    kd = ff // UK
    gu = 2 * kh
    stay = STAY * gu
    per_tick = nj * gu + nn * kd
    loop_units = per_tick - stay
    total = 2 * loop_units

    sec = lax.axis_index("section")
    ctx = lax.axis_index("ctx")
    dp = lax.axis_index("dp")
    core = ctx % 2
    ctx1 = ctx + 1 - 2 * core
    ctx2 = (ctx + 2) % 4
    ctx3 = 3 - ctx
    nxt = (sec + 1) % n_sec
    prv = (sec + n_sec - 1) % n_sec
    to_dp, to_c1, to_c2, to_c3 = {"dp": 1 - dp}, {"ctx": ctx1}, {"ctx": ctx2}, {"ctx": ctx3}
    to_next, to_prev = {"section": nxt}, {"section": prv}

    def load(slot, u):
        j, i = u // gu, u % gu
        rows = pl.ds(pl.multiple_of((i % kh) * UK, UK), UK)
        cols = pl.ds(pl.multiple_of(j * UN, UN), UN)

        @pl.when((u < nj * gu) & (i < kh))
        def _():
            pltpu.make_async_copy(wg.at[0, rows, cols], buf.at[slot], wsem.at[slot]).start()

        @pl.when((u < nj * gu) & (i >= kh))
        def _():
            pltpu.make_async_copy(wu.at[0, rows, cols], buf.at[slot], wsem.at[slot]).start()

        @pl.when(u >= nj * gu)
        def _():
            v = u - nj * gu
            n, k = v // kd, v % kd
            drows = pl.ds(pl.multiple_of(k * UK, UK), UK)
            dcols = pl.ds(pl.multiple_of(n * UN, UN), UN)
            pltpu.make_async_copy(wd.at[0, drows, dcols], buf.at[slot], wsem.at[slot]).start()

    def arrived(slot):
        pltpu.make_async_copy(
            wg.at[0, pl.ds(0, UK), pl.ds(0, UN)], buf.at[slot], wsem.at[slot]
        ).wait()

    def refill(q):
        later = q + RING

        @pl.when(later < total)
        def _():
            load(stay + q % RING, stay + later % loop_units)

    @pl.loop(0, stay + RING)
    def _(u):
        load(u, u)

    barrier = pltpu.get_barrier_semaphore()
    for where in (to_dp, to_c1, to_c2, to_c3, to_next, to_prev):
        pl.semaphore_signal(barrier, inc=1, device_id=where, device_id_type=MESH)

    diag = lax.broadcasted_iota(jnp.int32, (cap, cap), 0) == lax.broadcasted_iota(
        jnp.int32, (cap, cap), 1)
    lane_tok = lax.broadcasted_iota(jnp.int32, (cap, tok), 1).astype(F32)

    def column(row):
        spread = jnp.where(diag, jnp.broadcast_to(row.astype(F32), (cap, cap)), 0.0)
        return jnp.sum(spread, axis=1, keepdims=True)

    row0 = keeps[0]
    row1 = keeps[1]
    pick0 = (column(row0) == lane_tok).astype(BF16)
    klist[...] = jnp.full(klist.shape, -1, jnp.int32)
    klist[0:1, 0:cap] = row0
    for n in range(nn):
        xsend[n] = jnp.dot(
            pick0, stream[0, :, n * UN:(n + 1) * UN], preferred_element_type=F32
        ).astype(BF16)

    pl.semaphore_wait(barrier, 6)

    xcopy = rc(xsend, xrecv, misc_s.at[0], misc_r.at[0], to_dp)
    xcopy.start()
    kcopy = rc(klist, kprev, misc_s.at[1], misc_r.at[1], to_next)
    kcopy.start()
    scopy = rc(stream.at[0], pstream, misc_s.at[2], misc_r.at[2], to_next)
    scopy.start()
    bcopy = rc(b1send, b1recv, misc_s.at[3], misc_r.at[3], to_dp)
    mcopy = rc(msend, mrecv, misc_s.at[4], misc_r.at[4], to_dp)

    lane = lax.broadcasted_iota(jnp.int32, (cap, 128), 1)

    def stat_copy(t, p):
        return rc(stat_send, stat_recv.at[t, p], sts.at[p], strv.at[t, p],
                  (to_c1, to_c2, to_c3)[p])

    def c1copy(t, j):
        return rc(p1send.at[j], p1recv.at[t, j], p1s.at[j], p1r.at[t, j], to_c1)

    def c2copy(t, j):
        return rc(p2send.at[j], p2recv.at[t, j], p2s.at[j], p2r.at[t, j], to_c2)

    def c3copy(t, j):
        return rc(hid.at[t, j, core], hid.at[t, j, core], p3s.at[j], p3r.at[t, j], to_c1)

    def ucopy(t, n):
        return rc(usend.at[n], urecv.at[t, n], us.at[n], ur.at[t, n], to_dp)

    def ncopy(n):
        return rc(news.at[n], newr.at[n], ns.at[n], nr.at[n], to_next)

    for t in (0, 1):
        if t == 0:
            xcopy.wait_recv()
            for n in range(nn):
                xr[n] = xsend[n].astype(F32) + xrecv[n].astype(F32)
        else:
            bcopy.wait_recv()
            mcopy.wait_recv()
            match = (msend[...].astype(F32) + mrecv[...].astype(F32)).astype(BF16)[:, 0:cap]
            for n in range(nn):
                ncopy(n).wait_recv()
                xr[n] = (
                    b1send[n].astype(F32) + b1recv[n].astype(F32)
                    + jnp.dot(match, newr[n], preferred_element_type=F32)
                )
        ss = jnp.zeros((cap, 1), F32)
        lg = jnp.zeros((cap, 1), F32)
        for n in range(nn):
            block = xr[n]
            cols = slice(n * UN, (n + 1) * UN)
            ss += jnp.sum(block * block, axis=1, keepdims=True)
            lg += jnp.sum(block * router[0:1, cols].astype(F32), axis=1, keepdims=True)
            k, off = (n * UN) // UK, (n * UN) % UK
            xg[k, :, off:off + UN] = (block * gain[0:1, cols]).astype(BF16)
        stat_send[...] = jnp.where(lane < 64, ss, lg)
        for p in range(3):
            stat_copy(t, p).start()

        @pl.loop(0, nj + LAG)
        def _(s):
            @pl.when(s < nj)
            def _():
                def unit(i):
                    u = s * gu + i
                    q = t * loop_units + u - stay
                    slot = jnp.where(u < stay, u, stay + (q + RING * 8) % RING)
                    if t == 0:
                        arrived(slot)
                    else:
                        @pl.when(u >= stay)
                        def _():
                            arrived(slot)
                    return slot, u, q

                for which in range(2):
                    total_part = None
                    for k in range(kh):
                        slot, u, q = unit(which * kh + k)
                        term = jnp.dot(xg[k], buf[slot], preferred_element_type=F32)
                        total_part = term if total_part is None else total_part + term
                        refs = (u, q)

                        @pl.when(refs[0] >= stay)
                        def _():
                            refill(refs[1])
                    rows = slice(which * cap, (which + 1) * cap)
                    part[0, rows, :] = total_part[:, :HALF]
                    part[1, rows, :] = total_part[:, HALF:]
                own[s] = part[core]
                p1send[s] = part[1 - core].astype(BF16)
                c1copy(t, s).start()

            @pl.when((s >= 1) & (s < nj + 1))
            def _():
                j = s - 1
                c1copy(t, j).wait_recv()
                both = own[j] + p1recv[t, j].astype(F32)
                own[j] = both
                p2send[j] = both.astype(BF16)
                c2copy(t, j).start()

            @pl.when(s == LAG)
            def _():
                stats = stat_send[...]
                for p in range(3):
                    stat_copy(t, p).wait()
                    stats = stats + stat_recv[t, p]
                rs_b[...] = jnp.broadcast_to(
                    lax.rsqrt(stats[:, 0:1] / width + eps), rs_b.shape)
                sig_b[...] = jnp.broadcast_to(
                    1.0 / (1.0 + jnp.exp(-stats[:, 64:65])), sig_b.shape)

            @pl.when(s >= LAG)
            def _():
                j = s - LAG
                c2copy(t, j).wait_recv()
                both = own[j] + p2recv[t, j].astype(F32)
                scale = rs_b[:, 0:1]
                g = both[0:cap] * scale
                v = both[cap:2 * cap] * scale
                hid[t, j, core] = (g / (1.0 + jnp.exp(-g)) * v).astype(BF16)
                c3copy(t, j).start()

        if t == 0:
            kcopy.wait()
            scopy.wait()
            rowp = kprev[0:1, 0:cap]
            col1 = column(row1)
            same = (col1 == jnp.broadcast_to(rowp.astype(F32), (cap, cap))) & (col1 >= 0.0)
            same = same.astype(F32)
            fresh = jnp.sum(same, axis=1, keepdims=True) == 0.0
            pick1 = jnp.where(fresh, (col1 == lane_tok).astype(F32), 0.0).astype(BF16)
            msend[...] = jnp.zeros(msend.shape, BF16)
            msend[:, 0:cap] = same.astype(BF16)
            for n in range(nn):
                b1send[n] = jnp.dot(
                    pick1, pstream[:, n * UN:(n + 1) * UN], preferred_element_type=F32
                ).astype(BF16)
            bcopy.start()
            mcopy.start()
        else:
            row_tok = lax.broadcasted_iota(jnp.int32, (tok, cap), 0)
            place = (row_tok == jnp.broadcast_to(kprev[0:1, 0:cap], (tok, cap))).astype(F32)
            kept = jnp.sum(place, axis=1, keepdims=True) > 0.0
            place = place.astype(BF16)
            for n in range(nn):
                cols = slice(n * UN, (n + 1) * UN)
                moved = jnp.dot(place, newr[n], preferred_element_type=F32)
                out[0, :, cols] = jnp.where(
                    kept, moved, pstream[:, cols].astype(F32)).astype(BF16)

        @pl.loop(0, nj)
        def _(j):
            c1copy(t, j).wait_send()
            c2copy(t, j).wait_send()
            c3copy(t, j).wait()

        per = UK // UN

        @pl.loop(0, nn + 1)
        def _(n):
            @pl.when(n < nn)
            def _():
                acc = None
                for k in range(kd):
                    u = nj * gu + n * kd + k
                    q = t * loop_units + u - stay
                    slot = stay + q % RING
                    arrived(slot)
                    lhs = jnp.concatenate(
                        [hid[t, per * k + a, b] for a in range(per) for b in range(2)], axis=1)
                    term = jnp.dot(lhs, buf[slot], preferred_element_type=F32)
                    acc = term if acc is None else acc + term
                    refill(q)
                usend[n] = acc.astype(BF16)
                ucopy(t, n).start()

            @pl.when(n >= 1)
            def _():
                m = n - 1
                ucopy(t, m).wait()
                update = usend[m].astype(F32) + urecv[t, m].astype(F32)
                fresh_rows = (xr[m] + sig_b[:, 0:1] * update).astype(BF16)
                if t == 0:
                    news[m] = fresh_rows
                    ncopy(m).start()
                else:
                    mine = jnp.where(sec == 0, -1, row1)
                    spots = (
                        lax.broadcasted_iota(jnp.int32, (tok, cap), 0)
                        == jnp.broadcast_to(mine, (tok, cap))
                    ).astype(F32)
                    here = jnp.sum(spots, axis=1, keepdims=True) > 0.0
                    moved = jnp.dot(spots.astype(BF16), fresh_rows, preferred_element_type=F32)
                    cols = pl.ds(pl.multiple_of(m * UN, UN), UN)
                    out[0, :, cols] = jnp.where(
                        here, moved, out[0, :, cols].astype(F32)).astype(BF16)

    xcopy.wait_send()
    bcopy.wait_send()
    mcopy.wait_send()
    for n in range(nn):
        ncopy(n).wait_send()


def fused(n_sec, width, stream, norm_gain, w_router, w_gate, w_up, w_down, keep_rows):
    _, tok, feat = stream.shape
    ff = w_gate.shape[2]
    cap = keep_rows.shape[-1]
    gu = 2 * (feat // UK)
    nj, nn = ff // UN, feat // UN
    slots = STAY * gu + RING
    vm, dma = pltpu.VMEM, pltpu.SemaphoreType.DMA
    inside = pl.BlockSpec(memory_space=pltpu.VMEM)
    outside = pl.BlockSpec(memory_space=pl.ANY)
    units = ff * feat * 3
    return pl.pallas_call(
        functools.partial(kernel, (n_sec, cap, tok, feat, ff, width)),
        out_shape=jax.ShapeDtypeStruct(stream.shape, stream.dtype),
        in_specs=[inside] * 4 + [outside] * 3,
        out_specs=inside,
        scratch_shapes=[
            vm((slots, UK, UN), BF16),
            vm((tok, feat), BF16),
            vm((8, 128), jnp.int32),
            vm((8, 128), jnp.int32),
            vm((nn, cap, UN), BF16),
            vm((nn, cap, UN), BF16),
            vm((nn, cap, UN), F32),
            vm((feat // UK, cap, UK), BF16),
            vm((cap, 128), F32),
            vm((2, 3, cap, 128), F32),
            vm((cap, 128), F32),
            vm((cap, 128), F32),
            vm((2, 2 * cap, HALF), F32),
            vm((nj, 2 * cap, HALF), F32),
            vm((nj, 2 * cap, HALF), BF16),
            vm((2, nj, 2 * cap, HALF), BF16),
            vm((nj, 2 * cap, HALF), BF16),
            vm((2, nj, 2 * cap, HALF), BF16),
            vm((2, nj, 2, cap, HALF), BF16),
            vm((nn, cap, UN), BF16),
            vm((2, nn, cap, UN), BF16),
            vm((nn, cap, UN), BF16),
            vm((nn, cap, UN), BF16),
            vm((nn, cap, UN), BF16),
            vm((nn, cap, UN), BF16),
            vm((cap, 128), BF16),
            vm((cap, 128), BF16),
            dma((slots,)),
            dma((nj,)), dma((2, nj)), dma((nj,)), dma((2, nj)), dma((nj,)), dma((2, nj)),
            dma((nn,)), dma((2, nn)), dma((nn,)), dma((nn,)),
            dma((3,)), dma((2, 3)), dma((5,)), dma((5,)),
        ],
        compiler_params=pltpu.CompilerParams(
            collective_id=0, has_side_effects=True, vmem_limit_bytes=63 * 2**20),
        cost_estimate=pl.CostEstimate(
            flops=4 * cap * units, bytes_accessed=3 * units, transcendentals=0),
    )(stream, norm_gain, w_router, keep_rows[:, 0], w_gate, w_up, w_down)


def solution(mesh):
    shape = mesh.shape

    def body(stream, norm_gain, w_router, w_gate, w_up, w_down, keep_rows):
        args = (stream, norm_gain, w_router, w_gate, w_up, w_down, keep_rows)
        if shape["dp"] == 2 and shape["ctx"] == 4 and shape["section"] > 2:
            width = stream.shape[2] * shape["ctx"]
            return fused(shape["section"], width, *args)
        return local(*args)

    return jax.shard_map(
        body,
        mesh=mesh,
        in_specs=(
            P("section", "dp", "ctx"),
            P("section", "ctx"),
            P("section", "ctx"),
            P("section", "ctx", "dp"),
            P("section", "ctx", "dp"),
            P("section", "dp", "ctx"),
            P(None, "section", "dp", None),
        ),
        out_specs=P("section", "dp", "ctx"),
        check_vma=False,
    )
```

time: 326 us -> 89.8 us (0.28)
  waiting for transfers between devices: 190 us -> 0 us
  Pallas kernels: 0 us -> 87.8 us
  matrix products: 80.7 us -> 0 us
  blocking collectives: 25.8 us -> 0 us
  between operations: 13.3 us -> 0.01 us
  other arithmetic: 11.7 us -> 0 us
    psum x2 -> x0, waiting for transfers between devices: 153 us -> none  [hidden_block(): summed = lax.psum(partial_value, 'ctx')]
    pallas_call x0 -> x1, Pallas kernels: none -> 87.8 us  [fused(): pl.pallas_call(functools.partial(kernel, (n_sec, cap, tok, feat, ff, widt...]
    dot_general x6 -> x0, matrix products: 80.7 us -> none  [the longest x2 32.8 us: hidden_block(): jnp.dot(hidden, w_down, preferred_element_type=jnp.float32)]
    reduce_scatter x2 -> x0, waiting for transfers between devices: 23.7 us -> none  [hidden_block(): lax.psum_scatter(jnp.dot(hidden, w_down, preferred_element_type=jnp.float...]
    psum x2 -> x0, blocking collectives: 14 us -> none  [routed_layer(): squares, logits = lax.psum((squares, logits), 'ctx')]
    ppermute x1 -> x0, waiting for transfers between devices: 14 us -> none  [from_behind(): return lax.ppermute(value, axis, pairs)]
    all_gather x2 -> x0, blocking collectives: 11.7 us -> none  [hidden_block(): row_piece = lax.all_gather(normed, 'dp', axis=0, tiled=True)]
    another operation x2 -> x0, other arithmetic: 4.17 us -> none  [hidden_block(): partial_value = jnp.stack([gate_part, up_part], axis=1)]
  transfers between devices with their start and end apart: 5 -> 0, of which waited for: 5 -> 0; matrix products, arithmetic and copies ran while one was open for 0% -> 0% of each run, Pallas kernels for 0% -> 0%
where the time goes in v1:
time: 89.8 us; the launch traced here: 89.7 us
  Pallas kernels  87.8 us (98%)
  local copies, waits for them, and re-layouts  1.88 us (2%)
    pallas_call x1, Pallas kernels, fused(): pl.pallas_call(functools.partial(kernel, (n_sec, cap, tok, feat, ff, widt...  87.8 us
    unnamed x1, local copies, waits for them, and re-layouts  1.88 us

profile of v1, /device:TPU:0, one launch (start us, length us, event | category | flops | bytes accessed | tf_op | source)
XLA Modules:
  0.0 89.7 jit_solution(7424636678221976586)
XLA Ops:
  0.0 87.8 %shard_map.73 = bf16[1,128,2048]{2,1,0:T(8,128)(2,1)} custom-call(bf16[1,128,2048]{2,1,0:T(8,128)(2,1)} %stream.1, f32[1,2048]{1,0:T(1,128)} %gain.1, bf16[1,2048]{1,0:T(2,128)(2,1)} %router.1, s32[2,1,32]{2,1,0:T(1,128)} %bitcast.3, bf16[1,2048,7168]{2,1,0:T(8,128)(2,1)} %wg.1, bf16[1,2048,7168]{2,1,0:T(8,128)(2,1)} %wu.1, bf16[1,7168,2048]{2,1,0:T(8,128)(2,1)} %wd.1), custom_call_target="tpu_custom_call" | custom-call | flops 5637144576 | bytes 132120576 | tf_op jit(solution)/shard_map/pallas_call | solution.py:386
  87.8 1.9 %copy.10 = bf16[1,128,2048]{2,1,0:T(8,128)(2,1)} copy(bf16[1,128,2048]{2,1,0:T(8,128)(2,1)} %shard_map.73) | data formatting | bytes 1048576

commit v2 on v1

--- a/solution.py
+++ b/solution.py
@@ -229,35 +229,38 @@
         def _(s):
             @pl.when(s < nj)
             def _():
-                def unit(i):
+                units = []
+                for i in range(gu):
                     u = s * gu + i
                     q = t * loop_units + u - stay
-                    slot = jnp.where(u < stay, u, stay + (q + RING * 8) % RING)
-                    if t == 0:
+                    units.append((jnp.where(u < stay, u, stay + (q + RING * 8) % RING), q))
+
+                def wait_all():
+                    for slot, _ in units:
                         arrived(slot)
-                    else:
-                        @pl.when(u >= stay)
-                        def _():
-                            arrived(slot)
-                    return slot, u, q
+
+                if t == 0:
+                    wait_all()
+                else:
+                    pl.when(s >= STAY)(wait_all)
 
                 for which in range(2):
                     total_part = None
                     for k in range(kh):
-                        slot, u, q = unit(which * kh + k)
+                        slot = units[which * kh + k][0]
                         term = jnp.dot(xg[k], buf[slot], preferred_element_type=F32)
                         total_part = term if total_part is None else total_part + term
-                        refs = (u, q)
-
-                        @pl.when(refs[0] >= stay)
-                        def _():
-                            refill(refs[1])
                     rows = slice(which * cap, (which + 1) * cap)
                     part[0, rows, :] = total_part[:, :HALF]
                     part[1, rows, :] = total_part[:, HALF:]
                 own[s] = part[core]
                 p1send[s] = part[1 - core].astype(BF16)
                 c1copy(t, s).start()
+
+                @pl.when(s >= STAY)
+                def _():
+                    for _, q in units:
+                        refill(q)
 
             @pl.when((s >= 1) & (s < nj + 1))
             def _():
@@ -330,19 +333,20 @@
         def _(n):
             @pl.when(n < nn)
             def _():
+                first = t * loop_units + nj * gu + n * kd - stay
+                for k in range(kd):
+                    arrived(stay + (first + k) % RING)
                 acc = None
                 for k in range(kd):
-                    u = nj * gu + n * kd + k
-                    q = t * loop_units + u - stay
-                    slot = stay + q % RING
-                    arrived(slot)
                     lhs = jnp.concatenate(
                         [hid[t, per * k + a, b] for a in range(per) for b in range(2)], axis=1)
-                    term = jnp.dot(lhs, buf[slot], preferred_element_type=F32)
+                    term = jnp.dot(
+                        lhs, buf[stay + (first + k) % RING], preferred_element_type=F32)
                     acc = term if acc is None else acc + term
-                    refill(q)
                 usend[n] = acc.astype(BF16)
                 ucopy(t, n).start()
+                for k in range(kd):
+                    refill(first + k)
 
             @pl.when(n >= 1)
             def _():

time: 89.8 us -> 87.1 us (0.970)
  Pallas kernels: 87.8 us -> 85.1 us
    pallas_call x1, Pallas kernels: 87.8 us -> 85.1 us  [fused(): pl.pallas_call(functools.partial(kernel, (n_sec, cap, tok, feat, ff, widt...]
where the time goes in v2:
time: 87.1 us; the launch traced here: 86.9 us
  Pallas kernels  85.1 us (98%)
  local copies, waits for them, and re-layouts  1.88 us (2%)
    pallas_call x1, Pallas kernels, fused(): pl.pallas_call(functools.partial(kernel, (n_sec, cap, tok, feat, ff, widt...  85.1 us
    unnamed x1, local copies, waits for them, and re-layouts  1.88 us

profile of v2, /device:TPU:0, one launch (start us, length us, event | category | flops | bytes accessed | tf_op | source)
XLA Modules:
  0.0 86.9 jit_solution(4239170187828932340)
XLA Ops:
  0.0 85.1 %shard_map.73 = bf16[1,128,2048]{2,1,0:T(8,128)(2,1)} custom-call(bf16[1,128,2048]{2,1,0:T(8,128)(2,1)} %stream.1, f32[1,2048]{1,0:T(1,128)} %gain.1, bf16[1,2048]{1,0:T(2,128)(2,1)} %router.1, s32[2,1,32]{2,1,0:T(1,128)} %bitcast.3, bf16[1,2048,7168]{2,1,0:T(8,128)(2,1)} %wg.1, bf16[1,2048,7168]{2,1,0:T(8,128)(2,1)} %wu.1, bf16[1,7168,2048]{2,1,0:T(8,128)(2,1)} %wd.1), custom_call_target="tpu_custom_call" | custom-call | flops 5637144576 | bytes 132120576 | tf_op jit(solution)/shard_map/pallas_call | solution.py:390
  85.1 1.9 %copy.10 = bf16[1,128,2048]{2,1,0:T(8,128)(2,1)} copy(bf16[1,128,2048]{2,1,0:T(8,128)(2,1)} %shard_map.73) | data formatting | bytes 1048576
